TPU v7x, 32 devices: a whole 2x2x4 slice. The times are simulated.
32 devices in a mesh: groups: 2 (over x), ep: 16 (over z, y, core).
Axes of the slice: x: 2, y: 2, z: 4, core: 2. Of those that a mesh axis runs over, the one named last changes fastest.
Arguments:
- tokens: bfloat16 [1024, 3584], P(('groups', 'ep')), parts along dimension 0, may hold values from -6 to 6
- routes: int32 [1024, 8], P(('groups', 'ep')), parts along dimension 0, may hold values from 0 to 255, all different within a row; in each aligned block of 32 rows (0 to 31, 32 to 63, ...) at most 2 rows name the same one
- gate_num: int32 [1024, 8], P(('groups', 'ep')), parts along dimension 0, may hold values from 1 to 255
- w_gate: bfloat16 [16, 3584, 512], P('ep'), may hold values from -0.09375 to 0.09375
- w_up: bfloat16 [16, 3584, 512], P('ep'), may hold values from -0.09375 to 0.09375
- w_down: bfloat16 [16, 512, 3584], P('ep'), may hold values from -0.1875 to 0.1875
Outputs:
- combined: bfloat16 [1024, 3584], P(('groups', 'ep')), parts along dimension 0
There are 2 independent parts, one for each index of `groups`. A program takes and returns all parts, laid end to end along the dimension named above; an argument that names none is the same for every part. Nothing has to cross between parts.
Inputs may be any that keep to these rules, and one draw needn't show every extreme that they name: `routes`: each row names 8 different experts; among the 32 rows of one device no expert is named more than 2 times, a bound that some block reaches.
All inputs are finite; a program needn't handle non-finite values.
Results may differ from a plain program's by a relative error of at most 0.0058.
Values may be sent and summed in bfloat16 or wider, within the bound.
A program may use at most 64 MiB of HBM per device.

v0:
```python
import jax
import jax.numpy as jnp
from jax import lax
from jax.sharding import PartitionSpec as P

SPLIT = 2
EXPERTS = 256


def partner_2(block, axis, apart):
    count = lax.axis_size(axis)
    route = []
    for low in range(count):
        high = low | 1 << apart
        if high != low and high < count:
            route += [(low, high), (high, low)]
    return lax.ppermute(block, axis, route)


def expert_mlp(received, w_gate, w_up, w_down):
    local_count = w_gate.shape[0]
    senders = received.shape[0] // local_count
    slot_count = received.shape[1]
    feature_width = received.shape[2]
    blocks = received.reshape(senders, local_count, slot_count, feature_width)
    gate_part = jnp.einsum("secd,edf->secf", blocks, w_gate, preferred_element_type=jnp.float32)
    up_part = jnp.einsum("secd,edf->secf", blocks, w_up, preferred_element_type=jnp.float32)
    hidden = (jax.nn.silu(gate_part) * up_part).astype(jnp.bfloat16)
    output = jnp.einsum("secf,efd->secd", hidden, w_down, preferred_element_type=jnp.float32)
    return output.reshape(senders * local_count, slot_count, feature_width)


def serve_rows(received, w_gate, w_up, w_down):
    parity = lax.axis_index("ep") % 2
    partner = partner_2(received, "ep", 0)
    lower_rows = jnp.where(parity == 0, received, partner)
    upper_rows = jnp.where(parity == 0, partner, received)
    whole_rows = jnp.concatenate([lower_rows, upper_rows], axis=2)
    results = expert_mlp(whole_rows, w_gate, w_up, w_down)
    half_width = results.shape[2] // 2
    lower_out = results[:, :, :half_width]
    upper_out = results[:, :, half_width:]
    kept = jnp.where(parity == 0, lower_out, upper_out)
    sending = jnp.where(parity == 0, upper_out, lower_out)
    arrived = partner_2(sending, "ep", 0)
    summed = (kept + arrived).astype(jnp.bfloat16)
    return lax.all_to_all(summed, "ep", split_axis=0, concat_axis=0, tiled=True)


def shards(tokens, routes, gate_num, w_gate, w_up, w_down):
    tok_rows, top_count = routes.shape
    feature_width = tokens.shape[1]
    devices_all = lax.axis_size("ep")
    experts_all = devices_all // SPLIT
    capacity = max(2, min(tok_rows, 5 * tok_rows * top_count // (2 * EXPERTS)))
    flat_routes = routes.reshape(-1)
    served = flat_routes < experts_all
    one_hot = (flat_routes[:, None] == jnp.arange(experts_all, dtype=jnp.int32)[None, :]).astype(
        jnp.int32
    )
    before = jnp.cumsum(one_hot, axis=0) - one_hot
    position = jnp.sum(before * one_hot, axis=1)
    slot_total = experts_all * capacity
    slot_index = jnp.where(served, flat_routes * capacity + position, slot_total)
    token_of = jnp.arange(tok_rows * top_count, dtype=jnp.int32) // top_count
    source_row = jnp.zeros((slot_total,), jnp.int32).at[slot_index].set(token_of, mode="drop")
    filled = jnp.zeros((slot_total,), jnp.bool_).at[slot_index].set(True, mode="drop")
    outgoing = jnp.where(filled[:, None], tokens[source_row], jnp.zeros((), tokens.dtype))
    outgoing = outgoing.reshape(experts_all, capacity, feature_width)
    half_width = feature_width // SPLIT
    outgoing = outgoing.reshape(experts_all, capacity, SPLIT, half_width)
    outgoing = outgoing.transpose(0, 2, 1, 3).reshape(experts_all * SPLIT, capacity, half_width)
    received = lax.all_to_all(outgoing, "ep", split_axis=0, concat_axis=0, tiled=True)
    returned = serve_rows(received, w_gate, w_up, w_down)
    returned = returned.reshape(experts_all, SPLIT, capacity, half_width)
    expert_rows = returned.transpose(0, 2, 1, 3).reshape(experts_all, capacity, feature_width)
    safe_route = jnp.where(served, flat_routes, 0)
    picked = expert_rows[safe_route, position]
    picked = picked.reshape(tok_rows, top_count, feature_width)
    gate_real = jnp.where(
        served.reshape(tok_rows, top_count), gate_num.astype(jnp.float32) / 256.0, 0.0
    )
    weights = gate_real.astype(jnp.bfloat16)
    combined = jnp.einsum("tk,tkd->td", weights, picked, preferred_element_type=jnp.float32)
    return combined.astype(jnp.bfloat16)


def solution(mesh):
    return jax.shard_map(
        shards,
        mesh=mesh,
        in_specs=(
            P(("groups", "ep"), None),
            P(("groups", "ep"), None),
            P(("groups", "ep"), None),
            P("ep", None, None),
            P("ep", None, None),
            P("ep", None, None),
        ),
        out_specs=P(("groups", "ep"), None),
        check_vma=False,
    )
```

profile of v0, /device:TPU:0, one launch (start us, length us, event | category | flops | bytes accessed | tf_op | source)
XLA Modules:
  0.0 48.9 jit_solution(16190040157651471799)
XLA Ops:
  0.0 0.8 %copy.16 = s32[32,8]{1,0:T(8,128)S(1)} copy(s32[32,8]{0,1:T(8,128)} %param.7) | data formatting | bytes 2048 | tf_op args[1]
  0.8 0.1 eq.38
  1.1 0.6 %reduce-window.6 = s32[8,2,128]{2,0,1:T(8,128)S(1)} reduce-window(s32[8,2,128]{2,0,1:T(8,128)S(1)} %fusion.22, s32[]{:T(128)} %constant.50.clone.1), window={size=1x1x128 pad=0_0x0_0x127_0}, to_apply=%region_0.0 | reduce-window | flops 260096 | bytes 16388 | tf_op jit(solution)/shard_map/reduce-window
  1.7 0.2 slice_reduce_fusion
  1.9 0.1 fusion.21
  2.0 1.4 %scatter_custom_fusion.1 = s32[16]{0:T(128)S(1)} fusion(s32[256]{0:T(256)S(1)} %bitcast.73, s32[256]{0:T(256)S(1)} %and_select_fusion, s32[]{:T(128)} %constant.50.clone.1), kind=kCustom, calls=%fused_computation.52 | custom fusion | bytes 68 | tf_op jit(solution)/shard_map/scatter | solution.py:66
  3.5 1.5 %scatter_custom_fusion = pred[16]{0:T(512)(128)(4,1)S(1)} fusion(s32[256]{0:T(256)S(1)} %bitcast.74, pred[256]{0:T(512)(128)(4,1)S(1)} %broadcast.151, pred[]{:T(512)} %constant.53.clone.1), kind=kCustom, calls=%fused_computation.50 | custom fusion | bytes 17 | tf_op jit(solution)/shard_map/scatter | solution.py:67
  5.1 0.6 %gather_fusion = bf16[16,3584]{1,0:T(8,128)(2,1)S(1)} fusion(bf16[32,3584]{1,0:T(8,128)(2,1)S(1)} %copy-done, s32[1024]{0:T(1024)S(1)} %pad_clamp_fusion), kind=kCustom, calls=%fused_computation | custom fusion | bytes 229440 | tf_op jit(solution)/shard_map/gather | solution.py:68
  5.7 0.2 fusion.14
  5.9 0.1 copy.19
  6.0 14.9 %all_to_all.10 = bf16[16,2,1792]{2,1,0:T(2,128)(2,1)S(1)} all-to-all(bf16[16,2,1792]{2,1,0:T(2,128)(2,1)S(1)} %bitcast.70), channel_id=1, replica_groups=mesh['groups'=2,'ep'=16] {'ep'}, dimensions={0} | all-to-all | bytes 229376 | tf_op jit(solution)/shard_map/all_to_all | solution.py:73
  21.0 1.3 %collective-permute-done = bf16[16,2,1792]{2,0,1:T(8,128)(2,1)S(1)} collective-permute-done((bf16[16,2,1792]{2,0,1:T(8,128)(2,1)S(1)}, bf16[16,2,1792]{2,0,1:T(8,128)(2,1)S(1)}, u32[]{:S(2)}, u32[]{:S(2)}) %collective-permute-start) | collective-permute-done | bytes 114720 | tf_op jit(solution)/shard_map/ppermute | solution.py:17
  22.3 2.8 %fusion.8 = f32[16,1,2,512]{3,0,2,1:T(8,128)S(1)} fusion(bf16[1,3584,512]{2,1,0:T(8,128)(2,1)} %param.9, bf16[16,2,1792]{2,0,1:T(8,128)(2,1)S(1)} %get-tuple-element.6, bf16[16,2,1792]{2,0,1:T(8,128)(2,1)S(1)} %get-tuple-element.5), kind=kOutput, calls=%fused_computation.12 | convolution fusion | flops 117899264 | bytes 3964928 | tf_op jit(solution)/shard_map/secd,edf->secf/dot_general | solution.py:26
  25.1 4.6 %fusion = f32[16,2,3584]{2,0,1:T(8,128)S(1)} fusion(bf16[1,512,3584]{2,1,0:T(8,128)(2,1)} %param.11, f32[16,1,2,512]{3,0,2,1:T(8,128)S(1)} %fusion.8, bf16[1,3584,512]{2,1,0:T(8,128)(2,1)} %param.10, bf16[16,2,1792]{2,0,1:T(8,128)(2,1)S(1)} %get-tuple-element.6, bf16[16,2,1792]{2,0,1:T(8,128)(2,1)S(1)} %get-tuple-element.5), kind=kOutput, calls=%fused_computation.4 | convolution fusion | flops 235438080 | bytes 8093696 | tf_op jit(solution)/shard_map/secf,efd->secd/dot_general | solution.py:29
  29.7 0.2 collective-permute-start.1
  29.9 1.3 %collective-permute-done.1 = f32[16,2,1792]{2,0,1:T(8,128)S(1)} collective-permute-done((f32[16,2,1792]{2,0,1:T(8,128)S(1)}, f32[16,2,1792]{2,0,1:T(8,128)S(1)}, u32[]{:S(2)}, u32[]{:S(2)}) %collective-permute-start.1) | collective-permute-done | bytes 229408 | tf_op jit(solution)/shard_map/ppermute | solution.py:17
  31.3 0.7 %copy.23 = bf16[16,2,1792]{2,1,0:T(2,128)(2,1)} copy(bf16[16,2,1792]{2,0,1:T(8,128)(2,1)S(1)} %add_convert_fusion) | data formatting | bytes 229376 | tf_op jit(solution)/shard_map/convert_element_type | solution.py:46
  32.0 3.5 %all-to-all-start.1 = ((bf16[16,2,1792]{2,1,0:T(2,128)(2,1)}), bf16[16,2,1792]{2,1,0:T(2,128)(2,1)S(1)}, u32[]{:S(2)}, u32[]{:S(2)}) async-start(bf16[16,2,1792]{2,1,0:T(2,128)(2,1)} %copy.23), calls=%async_computation.1 | async-start | bytes 229376 | tf_op jit(solution)/shard_map/all_to_all | solution.py:47
  35.6 0.1 copy.25
  35.7 7.5 %all-to-all-done.1 = bf16[16,2,1792]{2,1,0:T(2,128)(2,1)S(1)} async-done(((bf16[16,2,1792]{2,1,0:T(2,128)(2,1)}), bf16[16,2,1792]{2,1,0:T(2,128)(2,1)S(1)}, u32[]{:S(2)}, u32[]{:S(2)}) %all-to-all-start.1) | async-done | bytes 114720 | tf_op jit(solution)/shard_map/all_to_all | solution.py:47
  43.2 0.1 copy.32
  43.4 4.1 %gather_fusion.1 = bf16[256,3584]{1,0:T(8,128)(2,1)S(1)} fusion(bf16[8,2,3584]{2,1,0:T(2,128)(2,1)S(1)} %reshape.142, s32[256]{0:T(256)S(1)} %bitcast.68), kind=kCustom, calls=%fused_computation.1 | custom fusion | bytes 3672064 | tf_op jit(solution)/shard_map/gather | solution.py:78
  47.5 0.6 %fusion.6 = bf16[32,1,3584]{2,1,0:T(2,128)(2,1)S(1)} fusion(bf16[32,8,1]{1,2,0:T(2,128)(2,1)S(1)} %copy.25, bf16[256,3584]{1,0:T(8,128)(2,1)S(1)} %gather_fusion.1), kind=kOutput, calls=%fused_computation.10 | convolution fusion | flops 1835008 | bytes 2064896 | tf_op jit(solution)/shard_map/tk,tkd->td/dot_general | solution.py:84
  48.1 0.7 %copy.31 = bf16[32,1,3584]{2,0,1:T(8,128)(2,1)} copy(bf16[32,1,3584]{2,1,0:T(2,128)(2,1)S(1)} %fusion.6) | data formatting | bytes 458752 | tf_op jit(solution)/shard_map/tk,tkd->td/dot_general | solution.py:84
  (25 shorter events, 0.6 us)
Async XLA Ops:
  0.0 5.1 %copy-start = (bf16[32,3584]{1,0:T(8,128)(2,1)S(1)}, bf16[32,3584]{1,0:T(8,128)(2,1)}, u32[]{:S(2)}) copy-start(bf16[32,3584]{1,0:T(8,128)(2,1)} %param.6) | copy-start | bytes 688132
  20.9 1.4 %collective-permute-start = (bf16[16,2,1792]{2,0,1:T(8,128)(2,1)S(1)}, bf16[16,2,1792]{2,0,1:T(8,128)(2,1)S(1)}, u32[]{:S(2)}, u32[]{:S(2)}) collective-permute-start(bf16[16,2,1792]{2,0,1:T(8,128)(2,1)S(1)} %copy.21), channel_id=1, source_target_pairs={{0,1},{1,0},{2,3},{3,2},{4,5},{5,4},{6,7},{7,6},{8,9},{9,8},{10,11... | collective-permute-start | bytes 344072 | tf_op jit(solution)/shard_map/ppermute | solution.py:17
  25.1 10.5 %copy-start.1 = (s32[32,8]{0,1:T(8,128)S(1)}, s32[32,8]{0,1:T(8,128)}, u32[]{:S(2)}) copy-start(s32[32,8]{0,1:T(8,128)} %param.7) | copy-start | bytes 3076
  25.1 10.5 %copy-start.2 = (s32[32,8]{0,1:T(8,128)S(1)}, s32[32,8]{0,1:T(8,128)}, u32[]{:S(2)}) copy-start(s32[32,8]{0,1:T(8,128)} %param.8) | copy-start | bytes 3076
  29.7 1.6 %collective-permute-start.1 = (f32[16,2,1792]{2,0,1:T(8,128)S(1)}, f32[16,2,1792]{2,0,1:T(8,128)S(1)}, u32[]{:S(2)}, u32[]{:S(2)}) collective-permute-start(f32[16,2,1792]{2,0,1:T(8,128)S(1)} %slice_select_fusion), channel_id=1, source_target_pairs={{0,1},{1,0},{2,3},{3,2},{4,5},{5,4},{6,7},{7,6},{8,9},{9,8},{10,11... | collective-permute-start | bytes 688136 | tf_op jit(solution)/shard_map/ppermute | solution.py:17
  32.0 11.2 %all-to-all-start.1 = ((bf16[16,2,1792]{2,1,0:T(2,128)(2,1)}), bf16[16,2,1792]{2,1,0:T(2,128)(2,1)S(1)}, u32[]{:S(2)}, u32[]{:S(2)}) async-start(bf16[16,2,1792]{2,1,0:T(2,128)(2,1)} %copy.23), calls=%async_computation.1 | async-start | bytes 229376 | tf_op jit(solution)/shard_map/all_to_all | solution.py:47
where the time goes:
time: 49.1 us; the launch traced here: 48.9 us
  blocking collectives  14.9 us (30%)
  local copies, waits for them, and re-layouts  10.9 us (22%)
  waiting for transfers between devices  10.1 us (21%)
  matrix products  7.98 us (16%)
  starting transfers between devices  3.8 us (8%)
  other arithmetic  1.01 us (2%)
    all_to_all x1, blocking collectives, shards(): lax.all_to_all(outgoing, 'ep', split_axis=0, concat_axis=0, tiled=True)  14.9 us
    all_to_all x1, waiting for transfers between devices, serve_rows(): return lax.all_to_all(summed, 'ep', split_axis=0, concat_axis=0, tiled=True)  7.51 us
    dot_general x1, matrix products, expert_mlp(): jnp.einsum('secf,efd->secd', hidden, w_down, preferred_element_type=jnp.f...  4.61 us
    gather x1, local copies, waits for them, and re-layouts, shards(): picked = expert_rows[safe_route, position]  4.12 us
    all_to_all x1, starting transfers between devices, serve_rows(): return lax.all_to_all(summed, 'ep', split_axis=0, concat_axis=0, tiled=True)  3.51 us
    dot_general x1, matrix products, expert_mlp(): jnp.einsum('secd,edf->secf', blocks, w_gate, preferred_element_type=jnp.f...  2.76 us
    ppermute x2, waiting for transfers between devices, partner_2(): return lax.ppermute(block, axis, route)  2.64 us
    scatter x1, local copies, waits for them, and re-layouts, shards(): jnp.zeros((slot_total,), jnp.bool_).at[slot_index].set(True, mode='drop')  1.49 us
  transfers between devices with their start and end apart: 3, of which 3 were waited for; matrix products, arithmetic and copies ran while one was open for 0% of the time, Pallas kernels for 0%

commit v1 on v0

v1 whole, which is shorter than its diff:
```python
import functools

import jax
import jax.numpy as jnp
from jax import lax
from jax.experimental import pallas as pl
from jax.experimental.pallas import tpu as pltpu
from jax.sharding import PartitionSpec as P

SPLIT = 2
CAP = 2
BLOCK = 256
TILE = 16
F32 = jnp.float32
BF16 = jnp.bfloat16


def iota(shape, dim):
    return lax.broadcasted_iota(jnp.int32, shape, dim)


def mm(a, b):
    return jnp.dot(a, b, preferred_element_type=F32)


def mm_nt(a, b):
    return lax.dot_general(a, b, (((1,), (1,)), ((), ())), preferred_element_type=F32)


def one_hot(cond):
    return jnp.where(cond, 1.0, 0.0).astype(BF16)


def kernel(
    n, group, tokens, routes, gates, wg_hbm, wu_hbm, wd_hbm, out,
    wg, wu, wd, send, recv, relayed, zsend, zrecv, rsend, ret,
    wsem, send_s, send_r, relay_s, relay_r, z_s, z_r, ret_s, ret_r,
):
    me = lax.axis_index("ep")
    side = lax.rem(me, SPLIT)
    partner = me + 1 - 2 * side
    rows, width = tokens.shape
    top = routes.shape[1]
    half = width // SPLIT
    blocks = half // BLOCK
    experts = n // SPLIT
    slots = experts * CAP

    loads = [
        pltpu.make_async_copy(src.at[0], dst, wsem.at[i])
        for i, (src, dst) in enumerate(((wg_hbm, wg), (wu_hbm, wu), (wd_hbm, wd)))
    ]
    for load in loads:
        load.start()

    barrier = pltpu.get_barrier_semaphore()

    def greet(step, carry):
        pl.semaphore_signal(
            barrier, inc=1, device_id={"ep": lax.rem(me + step, n)},
            device_id_type=pl.DeviceIdType.MESH,
        )
        return carry

    lax.fori_loop(1, n, greet, 0)

    slot_expert = iota((rows, slots), 1) // CAP
    named = jnp.zeros((rows, slots), F32)
    weight = jnp.zeros((rows, slots), F32)
    for k in range(top):
        hit = jnp.where(routes[:, k : k + 1] == slot_expert, 1.0, 0.0)
        named = named + hit
        weight = weight + hit * gates[:, k : k + 1].astype(F32)
    earlier = one_hot(iota((rows, rows), 1) < iota((rows, rows), 0))
    place = mm(earlier, named.astype(BF16))
    copy_of = lax.rem(iota((rows, slots), 1), CAP).astype(F32)
    chosen = jnp.where(place == copy_of, named, 0.0)
    scaled = chosen * weight * (1.0 / 256.0)

    packet_rows = experts * TILE
    spread = one_hot(
        (iota((packet_rows, slots), 0) // TILE * CAP + lax.rem(iota((packet_rows, slots), 0), CAP))
        == iota((packet_rows, slots), 1)
    )
    chosen_all = jnp.concatenate([chosen.astype(BF16)] * blocks, axis=0)
    shape = (packet_rows, blocks * rows)
    in_block = lax.rem(iota(shape, 0), TILE) // CAP == iota(shape, 1) // rows
    pick = jnp.where(in_block, mm_nt(spread, chosen_all), 0.0).astype(BF16)
    for h in range(SPLIT):
        stacked = jnp.concatenate(
            [tokens[:, h * half + b * BLOCK : h * half + (b + 1) * BLOCK] for b in range(blocks)],
            axis=0,
        )
        send[h] = mm(pick, stacked).astype(BF16).reshape(experts, TILE, BLOCK)

    pl.semaphore_wait(barrier, n - 1)

    def outgoing(dest):
        return pltpu.make_async_remote_copy(
            src_ref=send.at[lax.rem(dest, SPLIT), dest // SPLIT], dst_ref=recv.at[me],
            send_sem=send_s.at[dest], recv_sem=send_r.at[me],
            device_id={"ep": dest}, device_id_type=pl.DeviceIdType.MESH,
        )

    def incoming(src):
        return pltpu.make_async_remote_copy(
            src_ref=send.at[0, 0], dst_ref=recv.at[src],
            send_sem=send_s.at[src], recv_sem=send_r.at[src],
            device_id={"ep": src}, device_id_type=pl.DeviceIdType.MESH,
        )

    def relay(src):
        return pltpu.make_async_remote_copy(
            src_ref=recv.at[src], dst_ref=relayed.at[src],
            send_sem=relay_s.at[src], recv_sem=relay_r.at[src],
            device_id={"ep": partner}, device_id_type=pl.DeviceIdType.MESH,
        )

    def send_one(step, carry):
        outgoing(lax.rem(me + step, n)).start()
        return carry

    lax.fori_loop(1, n, send_one, 0)
    recv[me] = send[side, me // SPLIT]
    relay(me).start()

    def pass_on(step, carry):
        src = lax.rem(me + n - step, n)
        incoming(src).wait_recv()
        relay(src).start()
        return carry

    lax.fori_loop(1, n, pass_on, 0)

    shape = (blocks * group * CAP, group * TILE)
    line, col = iota(shape, 0), iota(shape, 1)
    source_row = lax.rem(line, group * CAP)
    gather = one_hot(
        col == source_row // CAP * TILE + line // (group * CAP) * CAP + lax.rem(source_row, CAP)
    )
    shape = shape[::-1]
    line, col = iota(shape, 1), iota(shape, 0)
    source_row = lax.rem(line, group * CAP)
    scatter = one_hot(
        col == source_row // CAP * TILE + line // (group * CAP) * CAP + lax.rem(source_row, CAP)
    )

    def unpack(ref):
        parts = []
        for g in range(n // group):
            flat = ref[g * group : (g + 1) * group].reshape(group * TILE, BLOCK)
            tall = mm(gather, flat).astype(BF16)
            parts.append(
                jnp.concatenate(
                    [tall[b * group * CAP : (b + 1) * group * CAP] for b in range(blocks)], axis=1
                )
            )
        return jnp.concatenate(parts, axis=0) if len(parts) > 1 else parts[0]

    own_rows = pl.ds(pl.multiple_of(side * half, BLOCK // 2), half)
    other_rows = pl.ds(pl.multiple_of((1 - side) * half, BLOCK // 2), half)
    mine = unpack(recv)
    loads[0].wait()
    gate_part = mm(mine, wg[own_rows, :])
    loads[1].wait()
    up_part = mm(mine, wu[own_rows, :])

    def relay_arrived(src, carry):
        relay(src).wait_recv()
        return carry

    lax.fori_loop(0, n, relay_arrived, 0)
    theirs = unpack(relayed)
    gate_part = gate_part + mm(theirs, wg[other_rows, :])
    up_part = up_part + mm(theirs, wu[other_rows, :])
    hidden = (gate_part / (1.0 + jnp.exp(-gate_part)) * up_part).astype(BF16)

    loads[2].wait()
    zsend[...] = mm(hidden, wd[:, other_rows])
    exchange = pltpu.make_async_remote_copy(
        src_ref=zsend, dst_ref=zrecv, send_sem=z_s, recv_sem=z_r,
        device_id={"ep": partner}, device_id_type=pl.DeviceIdType.MESH,
    )
    exchange.start()
    kept = mm(hidden, wd[:, own_rows])
    exchange.wait_recv()
    total = (kept + zrecv[...]).astype(BF16)
    for g in range(n // group):
        lines = slice(g * group * CAP, (g + 1) * group * CAP)
        tall = jnp.concatenate(
            [total[lines, b * BLOCK : (b + 1) * BLOCK] for b in range(blocks)], axis=0
        )
        rsend[g * group : (g + 1) * group] = (
            mm(scatter, tall).astype(BF16).reshape(group, TILE, BLOCK)
        )

    def give_back(dest):
        return pltpu.make_async_remote_copy(
            src_ref=rsend.at[dest], dst_ref=ret.at[side, me // SPLIT],
            send_sem=ret_s.at[dest], recv_sem=ret_r.at[me],
            device_id={"ep": dest}, device_id_type=pl.DeviceIdType.MESH,
        )

    def given(src):
        return pltpu.make_async_remote_copy(
            src_ref=rsend.at[src], dst_ref=ret.at[lax.rem(src, SPLIT), src // SPLIT],
            send_sem=ret_s.at[src], recv_sem=ret_r.at[src],
            device_id={"ep": src}, device_id_type=pl.DeviceIdType.MESH,
        )

    def return_one(step, carry):
        give_back(lax.rem(me + step, n)).start()
        return carry

    lax.fori_loop(1, n, return_one, 0)
    ret[side, me // SPLIT] = rsend[me]

    scaled_all = jnp.concatenate([scaled.astype(BF16)] * blocks, axis=0)
    shape = (blocks * rows, packet_rows)
    in_block = lax.rem(iota(shape, 1), TILE) // CAP == iota(shape, 0) // rows
    mix = jnp.where(in_block, mm_nt(scaled_all, spread), 0.0).astype(BF16)

    def drain(step, carry):
        other = lax.rem(me + step, n)
        outgoing(other).wait_send()
        relay(other).wait_send()
        return carry

    lax.fori_loop(1, n, drain, 0)
    relay(me).wait_send()
    exchange.wait_send()

    def returned(step, carry):
        given(lax.rem(me + n - step, n)).wait_recv()
        return carry

    lax.fori_loop(1, n, returned, 0)
    for h in range(SPLIT):
        tall = mm(mix, ret[h].reshape(packet_rows, BLOCK)).astype(BF16)
        for b in range(blocks):
            out[:, h * half + b * BLOCK : h * half + (b + 1) * BLOCK] = tall[
                b * rows : (b + 1) * rows
            ]

    def drain_back(step, carry):
        give_back(lax.rem(me + step, n)).wait_send()
        return carry

    lax.fori_loop(1, n, drain_back, 0)


def shards(tokens, routes, gate_num, w_gate, w_up, w_down):
    n = lax.axis_size("ep")
    rows, width = tokens.shape
    half = width // SPLIT
    experts = n // SPLIT
    group = min(n, 16)
    vmem = pl.BlockSpec(memory_space=pltpu.VMEM)
    hbm = pl.BlockSpec(memory_space=pl.ANY)
    sems = pltpu.SemaphoreType.DMA
    return pl.pallas_call(
        functools.partial(kernel, n, group),
        out_shape=jax.ShapeDtypeStruct((rows, width), BF16),
        in_specs=[vmem, vmem, vmem, hbm, hbm, hbm],
        out_specs=vmem,
        scratch_shapes=[
            pltpu.VMEM(w_gate.shape[1:], BF16),
            pltpu.VMEM(w_up.shape[1:], BF16),
            pltpu.VMEM(w_down.shape[1:], BF16),
            pltpu.VMEM((SPLIT, experts, TILE, BLOCK), BF16),
            pltpu.VMEM((n, TILE, BLOCK), BF16),
            pltpu.VMEM((n, TILE, BLOCK), BF16),
            pltpu.VMEM((n * CAP, half), F32),
            pltpu.VMEM((n * CAP, half), F32),
            pltpu.VMEM((n, TILE, BLOCK), BF16),
            pltpu.VMEM((SPLIT, experts, TILE, BLOCK), BF16),
            sems((3,)),
            sems((n,)), sems((n,)),
            sems((n,)), sems((n,)),
            sems, sems,
            sems((n,)), sems((n,)),
        ],
        compiler_params=pltpu.CompilerParams(
            collective_id=0, has_side_effects=True, vmem_limit_bytes=56 << 20
        ),
    )(tokens, routes, gate_num, w_gate, w_up, w_down)


def solution(mesh):
    return jax.shard_map(
        shards,
        mesh=mesh,
        in_specs=(
            P(("groups", "ep"), None),
            P(("groups", "ep"), None),
            P(("groups", "ep"), None),
            P("ep", None, None),
            P("ep", None, None),
            P("ep", None, None),
        ),
        out_specs=P(("groups", "ep"), None),
        check_vma=False,
    )
```

time: 49.1 us -> 27.8 us (0.57)
  Pallas kernels: 0 us -> 23.2 us
  blocking collectives: 14.9 us -> 0 us
  waiting for transfers between devices: 10.1 us -> 0 us
  matrix products: 7.98 us -> 0 us
  local copies, waits for them, and re-layouts: 10.9 us -> 4.37 us
  starting transfers between devices: 3.8 us -> 0 us
  other arithmetic: 1.01 us -> 0 us
    pallas_call x0 -> x1, Pallas kernels: none -> 23.2 us  [shards(): pl.pallas_call(functools.partial(kernel, n, group), out_shape=jax.ShapeDt...]
    all_to_all x1 -> x0, blocking collectives: 14.9 us -> none  [shards(): lax.all_to_all(outgoing, 'ep', split_axis=0, concat_axis=0, tiled=True)]
    dot_general x3 -> x0, matrix products: 7.98 us -> none  [the longest x1 4.61 us: expert_mlp(): jnp.einsum('secf,efd->secd', hidden, w_down, preferred_element_type=jnp.f...]
    all_to_all x1 -> x0, waiting for transfers between devices: 7.51 us -> none  [serve_rows(): return lax.all_to_all(summed, 'ep', split_axis=0, concat_axis=0, tiled=True)]
    gather x3 -> x0, local copies, waits for them, and re-layouts: 4.77 us -> none  [the longest x1 4.12 us: shards(): picked = expert_rows[safe_route, position]]
    unnamed x7 -> x3, local copies, waits for them, and re-layouts: 0.82 us -> 4.37 us
    all_to_all x1 -> x0, starting transfers between devices: 3.51 us -> none  [serve_rows(): return lax.all_to_all(summed, 'ep', split_axis=0, concat_axis=0, tiled=True)]
    scatter x2 -> x0, local copies, waits for them, and re-layouts: 2.88 us -> none  [the longest x1 1.49 us: shards(): jnp.zeros((slot_total,), jnp.bool_).at[slot_index].set(True, mode='drop')]
  transfers between devices with their start and end apart: 3 -> 0, of which waited for: 3 -> 0; matrix products, arithmetic and copies ran while one was open for 0% -> 0% of each run, Pallas kernels for 0% -> 0%
where the time goes in v1:
time: 27.8 us; the launch traced here: 27.6 us
  Pallas kernels  23.2 us (83%)
  local copies, waits for them, and re-layouts  4.37 us (16%)
    pallas_call x1, Pallas kernels, shards(): pl.pallas_call(functools.partial(kernel, n, group), out_shape=jax.ShapeDt...  23.2 us
    unnamed x3, local copies, waits for them, and re-layouts  4.37 us

profile of v1, /device:TPU:0, one launch (start us, length us, event | category | flops | bytes accessed | tf_op | source)
XLA Modules:
  0.0 27.6 jit_solution(16548571680528645052)
XLA Ops:
  0.0 1.4 %copy.7.routes = s32[32,8]{1,0:T(8,128)} copy(s32[32,8]{0,1:T(8,128)} %param.7) | data formatting | bytes 2048 | tf_op args[1]
  1.4 1.4 %copy.8.gates = s32[32,8]{1,0:T(8,128)} copy(s32[32,8]{0,1:T(8,128)} %param.8) | data formatting | bytes 2048 | tf_op args[2]
  2.7 23.2 %shard_map.64 = bf16[32,3584]{1,0:T(8,128)(2,1)} custom-call(bf16[32,3584]{1,0:T(8,128)(2,1)} %tokens.1, s32[32,8]{1,0:T(8,128)} %copy.7.routes, s32[32,8]{1,0:T(8,128)} %copy.8.gates, bf16[1,3584,512]{2,1,0:T(8,128)(2,1)} %wg_hbm.1, bf16[1,3584,512]{2,1,0:T(8,128)(2,1)} %wu_hbm.1, bf16[1,512,3584]{2,1,0:T(8,128)(2,1)} %wd_hbm.1), custom_call_target="tpu_custom_call" | custom-call | tf_op jit(solution)/shard_map/pallas_call | solution.py:261
  26.0 1.6 %copy.10 = bf16[32,3584]{1,0:T(8,128)(2,1)} copy(bf16[32,3584]{1,0:T(8,128)(2,1)} %shard_map.64) | data formatting | bytes 458752

commit v2 on v0

v2 whole, which is shorter than its diff:
```python
import functools

import jax
import jax.numpy as jnp
from jax import lax
from jax.experimental import pallas as pl
from jax.experimental.pallas import tpu as pltpu
from jax.sharding import PartitionSpec as P

SPLIT = 2
CAP = 2
BLOCK = 512
TILE = 16
F32 = jnp.float32
BF16 = jnp.bfloat16
MESH = pl.DeviceIdType.MESH


def iota(shape, dim):
    return lax.broadcasted_iota(jnp.int32, shape, dim)


def over(x, k):
    return x >> (k.bit_length() - 1) if k & (k - 1) == 0 else x // k


def mod(x, k):
    return x & (k - 1) if k & (k - 1) == 0 else x - x // k * k


def mm(a, b):
    return jnp.dot(a, b, preferred_element_type=F32)


def mm_nt(a, b):
    return lax.dot_general(a, b, (((1,), (1,)), ((), ())), preferred_element_type=F32)


def one_hot(cond):
    return jnp.where(cond, 1.0, 0.0).astype(BF16)


def packet_map(shape, group, line_dim):
    line, col = iota(shape, line_dim), iota(shape, 1 - line_dim)
    row = mod(line, group * CAP)
    return one_hot(col == over(row, CAP) * TILE + over(line, group * CAP) * CAP + mod(row, CAP))


def kernel(
    n, group, tokens_hbm, routes_hbm, gates_hbm, wg_hbm, wu_hbm, wd_hbm, ret, mix,
    tokens, routes, gates, wg, wu, wd, send, recv, relayed, kept, zsend, zrecv, rsend, gather, scatter,
    small_s, wsem, send_s, send_r, relay_s, relay_r, z_s, z_r, ret_s, ret_r,
):
    me = lax.axis_index("ep")
    side = lax.rem(me, SPLIT)
    here = me // SPLIT
    partner = me + 1 - 2 * side
    rows, width = tokens.shape
    top = routes.shape[0]
    blocks = width // BLOCK
    chips = n // SPLIT
    slots = chips * CAP
    half_rows = chips * CAP
    tiled_rows = blocks * rows

    barrier = pltpu.get_barrier_semaphore()

    def there(step):
        return lax.rem(here + step, chips)

    def greet(step, carry):
        pl.semaphore_signal(
            barrier, inc=1, device_id={"ep": there(step) * SPLIT + side}, device_id_type=MESH
        )
        return carry

    lax.fori_loop(1, chips, greet, 0)
    pl.semaphore_signal(barrier, inc=1, device_id={"ep": partner}, device_id_type=MESH)

    small = [
        pltpu.make_async_copy(src, dst, small_s.at[i])
        for i, (src, dst) in enumerate(
            ((routes_hbm, routes), (gates_hbm, gates), (tokens_hbm, tokens))
        )
    ]
    loads = [
        pltpu.make_async_copy(src.at[0], dst, wsem.at[i])
        for i, (src, dst) in enumerate(((wg_hbm, wg), (wu_hbm, wu), (wd_hbm, wd)))
    ]
    for load in small + loads:
        load.start()

    shape = (rows, tiled_rows)
    token_of = mod(iota(shape, 1), rows)
    repeat = one_hot(token_of == iota(shape, 0))
    earlier = one_hot(iota(shape, 0) < token_of)
    packet_rows = chips * TILE
    shape = (packet_rows, slots)
    line = iota(shape, 0)
    spread = one_hot(over(line, TILE) * CAP + mod(line, CAP) == iota(shape, 1))
    shape = (packet_rows, tiled_rows)
    in_block = over(mod(iota(shape, 0), TILE), CAP) == over(iota(shape, 1), rows)
    shape = (slots, tiled_rows)
    expert_of = over(iota(shape, 0), CAP).astype(F32)
    copy_of = mod(iota(shape, 0), CAP).astype(F32)
    small[0].wait()
    small[1].wait()
    ints = jnp.concatenate([routes[...], gates[...]], axis=0).astype(F32).astype(BF16)
    tiled = mm(ints, repeat)
    named = jnp.zeros(shape, F32)
    weight = jnp.zeros(shape, F32)
    for k in range(top):
        hit = tiled[k : k + 1] == expert_of
        named = jnp.where(hit, 1.0, named)
        weight = jnp.where(hit, tiled[top + k : top + k + 1], weight)
    place = mm(named[:, :rows].astype(BF16), earlier)
    chosen = jnp.where(place == copy_of, named, 0.0)

    pick = jnp.where(in_block, mm(spread, chosen.astype(BF16)), 0.0).astype(BF16)
    small[2].wait()
    stacked = jnp.concatenate(
        [tokens[:, b * BLOCK : (b + 1) * BLOCK] for b in range(blocks)], axis=0
    )
    send[...] = mm(pick, stacked).astype(BF16).reshape(chips, TILE, BLOCK)

    pl.semaphore_wait(barrier, chips)

    def outgoing(q):
        return pltpu.make_async_remote_copy(
            src_ref=send.at[q], dst_ref=recv.at[here], send_sem=send_s.at[q],
            recv_sem=send_r.at[here], device_id={"ep": q * SPLIT + side}, device_id_type=MESH,
        )

    def incoming(q):
        return pltpu.make_async_remote_copy(
            src_ref=send.at[q], dst_ref=recv.at[q], send_sem=send_s.at[q],
            recv_sem=send_r.at[q], device_id={"ep": q * SPLIT + side}, device_id_type=MESH,
        )

    def relay(q):
        return pltpu.make_async_remote_copy(
            src_ref=recv.at[q], dst_ref=relayed.at[q], send_sem=relay_s.at[q],
            recv_sem=relay_r.at[q], device_id={"ep": partner}, device_id_type=MESH,
        )

    def send_one(step, carry):
        outgoing(there(step)).start()
        return carry

    lax.fori_loop(1, chips, send_one, 0)
    recv[here] = send[here]
    relay(here).start()

    gather[...] = packet_map((blocks * group * CAP, group * TILE), group, 0)
    scatter[...] = packet_map((group * TILE, blocks * group * CAP), group, 1)
    scaled = (chosen * weight * (1.0 / 256.0)).astype(BF16)
    pick_scaled = jnp.where(in_block, mm(spread, scaled), 0.0).astype(BF16)
    shape = (tiled_rows, tiled_rows)
    mix[...] = mm_nt(one_hot(iota(shape, 0) == iota(shape, 1)), pick_scaled).astype(BF16)

    def pass_on(step, carry):
        q = there(chips - step)
        incoming(q).wait_recv()
        relay(q).start()
        return carry

    lax.fori_loop(1, chips, pass_on, 0)

    def unpack(ref):
        parts = []
        for g in range(chips // group):
            flat = ref[g * group : (g + 1) * group].reshape(group * TILE, BLOCK)
            tall = mm(gather[...], flat).astype(BF16)
            step = group * CAP
            parts.append(
                jnp.concatenate([tall[b * step : (b + 1) * step] for b in range(blocks)], axis=1)
            )
        return parts

    mine = unpack(recv)
    loads[0].wait()
    loads[1].wait()

    def relay_arrived(step, carry):
        relay(there(step)).wait_recv()
        return carry

    lax.fori_loop(0, chips, relay_arrived, 0)
    x = jnp.concatenate(mine + unpack(relayed), axis=0)
    gate_part = mm(x, wg[...])
    up_part = mm(x, wu[...])
    hidden = (gate_part / (1.0 + jnp.exp(-gate_part)) * up_part).astype(BF16)

    def exchange(b):
        return pltpu.make_async_remote_copy(
            src_ref=zsend.at[b], dst_ref=zrecv.at[b], send_sem=z_s.at[b], recv_sem=z_r.at[b],
            device_id={"ep": partner}, device_id_type=MESH,
        )

    loads[2].wait()
    for b in range(blocks):
        z = mm(hidden, wd[:, b * BLOCK : (b + 1) * BLOCK])
        zsend[b] = z[half_rows:]
        exchange(b).start()
        kept[b] = z[:half_rows]
    total = []
    for b in range(blocks):
        exchange(b).wait_recv()
        total.append((kept[b] + zrecv[b]).astype(BF16))
    for g in range(chips // group):
        lines = slice(g * group * CAP, (g + 1) * group * CAP)
        tall = jnp.concatenate([part[lines] for part in total], axis=0)
        packed = mm(scatter[...], tall).astype(BF16)
        rsend[g * group : (g + 1) * group] = packed.reshape(group, TILE, BLOCK)

    def give_back(q):
        return pltpu.make_async_remote_copy(
            src_ref=rsend.at[q], dst_ref=ret.at[here], send_sem=ret_s.at[q],
            recv_sem=ret_r.at[here], device_id={"ep": q * SPLIT + side}, device_id_type=MESH,
        )

    def given(q):
        return pltpu.make_async_remote_copy(
            src_ref=rsend.at[q], dst_ref=ret.at[q], send_sem=ret_s.at[q],
            recv_sem=ret_r.at[q], device_id={"ep": q * SPLIT + side}, device_id_type=MESH,
        )

    def return_one(step, carry):
        give_back(there(step)).start()
        return carry

    lax.fori_loop(1, chips, return_one, 0)
    ret[here] = rsend[here]

    def drain(step, carry):
        outgoing(there(step)).wait_send()
        relay(there(step)).wait_send()
        return carry

    lax.fori_loop(1, chips, drain, 0)
    relay(here).wait_send()
    for b in range(blocks):
        exchange(b).wait_send()

    def returned(step, carry):
        given(there(chips - step)).wait_recv()
        return carry

    lax.fori_loop(1, chips, returned, 0)

    def drain_back(step, carry):
        give_back(there(step)).wait_send()
        return carry

    lax.fori_loop(1, chips, drain_back, 0)


def combine(ret, mix, out):
    rows = out.shape[0]
    chips = ret.shape[0]
    tall = mm(mix[...], ret[...].reshape(chips * TILE, BLOCK)).astype(BF16)
    for b in range(out.shape[1] // BLOCK):
        out[:, b * BLOCK : (b + 1) * BLOCK] = tall[b * rows : (b + 1) * rows]


def shards(tokens, routes, gate_num, w_gate, w_up, w_down):
    n = lax.axis_size("ep")
    rows, width = tokens.shape
    top = routes.shape[1]
    chips = n // SPLIT
    blocks = width // BLOCK
    group = min(chips, 8)
    half_rows = chips * CAP
    vmem = pl.BlockSpec(memory_space=pltpu.VMEM)
    hbm = pl.BlockSpec(memory_space=pl.ANY)
    sems = pltpu.SemaphoreType.DMA
    ret, mix = pl.pallas_call(
        functools.partial(kernel, n, group),
        out_shape=[
            jax.ShapeDtypeStruct((chips, TILE, BLOCK), BF16),
            jax.ShapeDtypeStruct((blocks * rows, chips * TILE), BF16),
        ],
        in_specs=[hbm] * 6,
        out_specs=[vmem, vmem],
        scratch_shapes=[
            pltpu.VMEM((rows, width), BF16),
            pltpu.VMEM((top, rows), jnp.int32),
            pltpu.VMEM((top, rows), jnp.int32),
            pltpu.VMEM(w_gate.shape[1:], BF16),
            pltpu.VMEM(w_up.shape[1:], BF16),
            pltpu.VMEM(w_down.shape[1:], BF16),
            pltpu.VMEM((chips, TILE, BLOCK), BF16),
            pltpu.VMEM((chips, TILE, BLOCK), BF16),
            pltpu.VMEM((chips, TILE, BLOCK), BF16),
            pltpu.VMEM((blocks, half_rows, BLOCK), F32),
            pltpu.VMEM((blocks, half_rows, BLOCK), F32),
            pltpu.VMEM((blocks, half_rows, BLOCK), F32),
            pltpu.VMEM((chips, TILE, BLOCK), BF16),
            pltpu.VMEM((blocks * group * CAP, group * TILE), BF16),
            pltpu.VMEM((group * TILE, blocks * group * CAP), BF16),
            sems((3,)),
            sems((3,)),
            sems((chips,)), sems((chips,)),
            sems((chips,)), sems((chips,)),
            sems((blocks,)), sems((blocks,)),
            sems((chips,)), sems((chips,)),
        ],
        compiler_params=pltpu.CompilerParams(
            collective_id=0, has_side_effects=True, vmem_limit_bytes=56 << 20
        ),
    )(tokens, routes.T, gate_num.T, w_gate, w_up, w_down)
    return pl.pallas_call(
        combine,
        out_shape=jax.ShapeDtypeStruct((rows, width), BF16),
        in_specs=[vmem, vmem],
        out_specs=vmem,
    )(ret, mix)


def solution(mesh):
    return jax.shard_map(
        shards,
        mesh=mesh,
        in_specs=(
            P(("groups", "ep"), None),
            P(("groups", "ep"), None),
            P(("groups", "ep"), None),
            P("ep", None, None),
            P("ep", None, None),
            P("ep", None, None),
        ),
        out_specs=P(("groups", "ep"), None),
        check_vma=False,
    )
```

time: 49.1 us -> 23.4 us (0.48)
  Pallas kernels: 0 us -> 23.3 us
  blocking collectives: 14.9 us -> 0 us
  local copies, waits for them, and re-layouts: 10.9 us -> 0 us
  waiting for transfers between devices: 10.1 us -> 0 us
  matrix products: 7.98 us -> 0 us
  starting transfers between devices: 3.8 us -> 0 us
  other arithmetic: 1.01 us -> 0 us
    pallas_call x0 -> x2, Pallas kernels: none -> 23.3 us  [the longest x1 21.5 us: shards(): pl.pallas_call(functools.partial(kernel, n, group), out_shape=[jax.ShapeD...]
    all_to_all x1 -> x0, blocking collectives: 14.9 us -> none  [shards(): lax.all_to_all(outgoing, 'ep', split_axis=0, concat_axis=0, tiled=True)]
    dot_general x3 -> x0, matrix products: 7.98 us -> none  [the longest x1 4.61 us: expert_mlp(): jnp.einsum('secf,efd->secd', hidden, w_down, preferred_element_type=jnp.f...]
    all_to_all x1 -> x0, waiting for transfers between devices: 7.51 us -> none  [serve_rows(): return lax.all_to_all(summed, 'ep', split_axis=0, concat_axis=0, tiled=True)]
    gather x3 -> x0, local copies, waits for them, and re-layouts: 4.77 us -> none  [the longest x1 4.12 us: shards(): picked = expert_rows[safe_route, position]]
    all_to_all x1 -> x0, starting transfers between devices: 3.51 us -> none  [serve_rows(): return lax.all_to_all(summed, 'ep', split_axis=0, concat_axis=0, tiled=True)]
    scatter x2 -> x0, local copies, waits for them, and re-layouts: 2.88 us -> none  [the longest x1 1.49 us: shards(): jnp.zeros((slot_total,), jnp.bool_).at[slot_index].set(True, mode='drop')]
    ppermute x2 -> x0, waiting for transfers between devices: 2.64 us -> none  [partner_2(): return lax.ppermute(block, axis, route)]
  transfers between devices with their start and end apart: 3 -> 0, of which waited for: 3 -> 0; matrix products, arithmetic and copies ran while one was open for 0% -> 0% of each run, Pallas kernels for 0% -> 0%
where the time goes in v2:
time: 23.4 us; the launch traced here: 23.3 us
  Pallas kernels  23.3 us (100%)
    pallas_call x1, Pallas kernels, shards(): pl.pallas_call(functools.partial(kernel, n, group), out_shape=[jax.ShapeD...  21.5 us
    pallas_call x1, Pallas kernels, shards(): pl.pallas_call(combine, out_shape=jax.ShapeDtypeStruct((rows, width), BF1...  1.8 us

profile of v2, /device:TPU:0, one launch (start us, length us, event | category | flops | bytes accessed | tf_op | source)
XLA Modules:
  0.0 23.3 jit_solution(16948905999394962556)
XLA Ops:
  0.0 21.5 %shard_map.64 = (bf16[8,16,512]{2,1,0:T(8,128)(2,1)}, bf16[224,128]{1,0:T(8,128)(2,1)}) custom-call(bf16[32,3584]{1,0:T(8,128)(2,1)} %tokens_hbm.1, s32[8,32]{1,0:T(8,128)} %bitcast.2, s32[8,32]{1,0:T(8,128)} %bitcast.3, bf16[1,3584,512]{2,1,0:T(8,128)(2,1)} %wg_hbm.1, bf16[1,3584,512]{2,1,0:T(8,128)(2,1)} %wu_hbm.1, bf16[1,512,3584]{2,1,0:T(8,128)(2,1)} %wd_hbm.1), custom_call_target="tpu_custom_call" | custom-call | tf_op jit(solution)/shard_map/pallas_call | solution.py:277
  21.5 1.8 %shard_map.65 = bf16[32,3584]{1,0:T(8,128)(2,1)} custom-call(bf16[8,16,512]{2,1,0:T(8,128)(2,1)} %get-tuple-element.7.ret, bf16[224,128]{1,0:T(8,128)(2,1)} %get-tuple-element.8.mix), custom_call_target="tpu_custom_call" | custom-call | tf_op jit(solution)/shard_map/pallas_call | solution.py:312

commit v3 on v2

v3 whole, which is shorter than its diff:
```python
import functools

import jax
import jax.numpy as jnp
from jax import lax
from jax.experimental import pallas as pl
from jax.experimental.pallas import tpu as pltpu
from jax.sharding import PartitionSpec as P

SPLIT = 2
CAP = 2
BLOCK = 256
PARTS = 2
TILE = 16
F32 = jnp.float32
BF16 = jnp.bfloat16
MESH = pl.DeviceIdType.MESH


def iota(shape, dim):
    return lax.broadcasted_iota(jnp.int32, shape, dim)


def over(x, k):
    return x >> (k.bit_length() - 1) if k & (k - 1) == 0 else x // k


def mod(x, k):
    return x & (k - 1) if k & (k - 1) == 0 else x - x // k * k


def mm(a, b):
    return jnp.dot(a, b, preferred_element_type=F32)


def mm_nt(a, b):
    return lax.dot_general(a, b, (((1,), (1,)), ((), ())), preferred_element_type=F32)


def one_hot(cond):
    return jnp.where(cond, 1.0, 0.0).astype(BF16)


def packet_map(shape, group, line_dim):
    line, col = iota(shape, line_dim), iota(shape, 1 - line_dim)
    row = mod(line, group * CAP)
    return one_hot(col == over(row, CAP) * TILE + over(line, group * CAP) * CAP + mod(row, CAP))


def kernel(
    n, group, tokens, routes, gates, wg_hbm, wu_hbm, wd_hbm, ret, mix,
    wg, wu, wd, send, recv, relayed, kept, zsend, zrecv, rsend, gather, scatter, wsem, send_s, send_r, relay_s, relay_r, z_s, z_r, ret_s, ret_r,
):
    me = lax.axis_index("ep")
    side = lax.rem(me, SPLIT)
    here = me // SPLIT
    partner = me + 1 - 2 * side
    rows, width = tokens.shape
    top = routes.shape[0]
    part = width // PARTS
    blocks = part // BLOCK
    chips = n // SPLIT
    slots = chips * CAP
    half_rows = chips * CAP
    tiled_rows = blocks * rows

    barrier = pltpu.get_barrier_semaphore()

    middle = chips // 2
    base = here // middle * middle

    def others(act, back=False):
        def across(step, carry):
            act(middle - base + lax.rem(here + (middle - step if back else step), middle))
            return carry

        def beside(step, carry):
            act(base + lax.rem(here + (middle - step if back else step), middle))
            return carry

        lax.fori_loop(0, middle, across, 0)
        lax.fori_loop(1, middle, beside, 0)

    def greet(q):
        pl.semaphore_signal(
            barrier, inc=1, device_id={"ep": q * SPLIT + side}, device_id_type=MESH
        )

    others(greet)
    pl.semaphore_signal(barrier, inc=1, device_id={"ep": partner}, device_id_type=MESH)

    loads = [
        pltpu.make_async_copy(src.at[0], dst, wsem.at[i])
        for i, (src, dst) in enumerate(((wg_hbm, wg), (wu_hbm, wu), (wd_hbm, wd)))
    ]
    for load in loads:
        load.start()

    shape = (rows, tiled_rows)
    token_of = mod(iota(shape, 1), rows)
    repeat = one_hot(token_of == iota(shape, 0))
    earlier = one_hot(iota(shape, 0) < token_of)
    packet_rows = chips * TILE
    shape = (packet_rows, slots)
    line = iota(shape, 0)
    spread = one_hot(over(line, TILE) * CAP + mod(line, CAP) == iota(shape, 1))
    shape = (packet_rows, tiled_rows)
    in_block = over(mod(iota(shape, 0), TILE), CAP) == over(iota(shape, 1), rows)
    shape = (slots, tiled_rows)
    expert_of = over(iota(shape, 0), CAP).astype(F32)
    copy_of = mod(iota(shape, 0), CAP).astype(F32)
    ints = jnp.concatenate([routes[...], gates[...]], axis=0).astype(F32).astype(BF16)
    tiled = mm(ints, repeat)
    named = jnp.zeros(shape, F32)
    weight = jnp.zeros(shape, F32)
    for k in range(top):
        hit = tiled[k : k + 1] == expert_of
        named = jnp.where(hit, 1.0, named)
        weight = jnp.where(hit, tiled[top + k : top + k + 1], weight)
    place = mm(named[:, :rows].astype(BF16), earlier)
    chosen = jnp.where(place == copy_of, named, 0.0)

    pick = jnp.where(in_block, mm(spread, chosen.astype(BF16)), 0.0).astype(BF16)

    def outgoing(h, q):
        return pltpu.make_async_remote_copy(
            src_ref=send.at[h, q], dst_ref=recv.at[h, here], send_sem=send_s.at[h, q],
            recv_sem=send_r.at[h, here], device_id={"ep": q * SPLIT + side}, device_id_type=MESH,
        )

    def incoming(h, q):
        return pltpu.make_async_remote_copy(
            src_ref=send.at[h, q], dst_ref=recv.at[h, q], send_sem=send_s.at[h, q],
            recv_sem=send_r.at[h, q], device_id={"ep": q * SPLIT + side}, device_id_type=MESH,
        )

    def relay(h, q):
        return pltpu.make_async_remote_copy(
            src_ref=recv.at[h, q], dst_ref=relayed.at[h, q], send_sem=relay_s.at[h, q],
            recv_sem=relay_r.at[h, q], device_id={"ep": partner}, device_id_type=MESH,
        )

    for h in range(PARTS):
        stacked = jnp.concatenate(
            [tokens[:, h * part + b * BLOCK : h * part + (b + 1) * BLOCK] for b in range(blocks)],
            axis=0,
        )
        send[h] = mm(pick, stacked).astype(BF16).reshape(chips, TILE, BLOCK)
        if h == 0:
            pl.semaphore_wait(barrier, chips)
        others(lambda q: outgoing(h, q).start())
    for h in range(PARTS):
        recv[h, here] = send[h, here]
        relay(h, here).start()

    gather[...] = packet_map((blocks * group * CAP, group * TILE), group, 0)
    scatter[...] = packet_map((group * TILE, blocks * group * CAP), group, 1)
    scaled = (chosen * weight * (1.0 / 256.0)).astype(BF16)
    pick_scaled = jnp.where(in_block, mm(spread, scaled), 0.0).astype(BF16)
    shape = (tiled_rows, tiled_rows)
    mix[...] = mm_nt(one_hot(iota(shape, 0) == iota(shape, 1)), pick_scaled).astype(BF16)

    def unpack(ref, h):
        parts = []
        step = group * CAP
        for g in range(chips // group):
            flat = ref[h, g * group : (g + 1) * group].reshape(group * TILE, BLOCK)
            tall = mm(gather[...], flat).astype(BF16)
            parts.append(
                jnp.concatenate([tall[b * step : (b + 1) * step] for b in range(blocks)], axis=1)
            )
        return parts

    for h in range(PARTS):

        def pass_on(q):
            incoming(h, q).wait_recv()
            relay(h, q).start()

        others(pass_on, back=True)

    loads[0].wait()
    loads[1].wait()
    gate_part = up_part = None
    for h in range(PARTS):
        relay(h, here).wait_recv()
        others(lambda q: relay(h, q).wait_recv(), back=True)
        x = jnp.concatenate(unpack(recv, h) + unpack(relayed, h), axis=0)
        gate_more = mm(x, wg[h * part : (h + 1) * part])
        up_more = mm(x, wu[h * part : (h + 1) * part])
        gate_part = gate_more if h == 0 else gate_part + gate_more
        up_part = up_more if h == 0 else up_part + up_more
    hidden = (gate_part / (1.0 + jnp.exp(-gate_part)) * up_part).astype(BF16)

    def exchange(h):
        return pltpu.make_async_remote_copy(
            src_ref=zsend.at[h], dst_ref=zrecv.at[h], send_sem=z_s.at[h], recv_sem=z_r.at[h],
            device_id={"ep": partner}, device_id_type=MESH,
        )

    def give_back(h, q):
        return pltpu.make_async_remote_copy(
            src_ref=rsend.at[h, q], dst_ref=ret.at[h, here], send_sem=ret_s.at[h, q],
            recv_sem=ret_r.at[h, here], device_id={"ep": q * SPLIT + side}, device_id_type=MESH,
        )

    def given(h, q):
        return pltpu.make_async_remote_copy(
            src_ref=rsend.at[h, q], dst_ref=ret.at[h, q], send_sem=ret_s.at[h, q],
            recv_sem=ret_r.at[h, q], device_id={"ep": q * SPLIT + side}, device_id_type=MESH,
        )

    loads[2].wait()
    for h in range(PARTS):
        z = mm(hidden, wd[:, h * part : (h + 1) * part])
        zsend[h] = z[half_rows:]
        exchange(h).start()
        kept[h] = z[:half_rows]
    for h in range(PARTS):
        exchange(h).wait_recv()
        total = (kept[h] + zrecv[h]).astype(BF16)
        for g in range(chips // group):
            lines = slice(g * group * CAP, (g + 1) * group * CAP)
            tall = jnp.concatenate(
                [total[lines, b * BLOCK : (b + 1) * BLOCK] for b in range(blocks)], axis=0
            )
            packed = mm(scatter[...], tall).astype(BF16)
            rsend[h, g * group : (g + 1) * group] = packed.reshape(group, TILE, BLOCK)
        others(lambda q: give_back(h, q).start())
        ret[h, here] = rsend[h, here]

    for h in range(PARTS):

        def sent(q):
            outgoing(h, q).wait_send()
            relay(h, q).wait_send()

        others(sent)
        relay(h, here).wait_send()
        exchange(h).wait_send()
    for h in range(PARTS):
        others(lambda q: given(h, q).wait_recv(), back=True)
    for h in range(PARTS):
        others(lambda q: give_back(h, q).wait_send())


def combine(ret, mix, out):
    rows = out.shape[0]
    chips = ret.shape[1]
    part = out.shape[1] // PARTS
    for h in range(PARTS):
        tall = mm(mix[...], ret[h].reshape(chips * TILE, BLOCK)).astype(BF16)
        for b in range(part // BLOCK):
            at = h * part + b * BLOCK
            out[:, at : at + BLOCK] = tall[b * rows : (b + 1) * rows]


def shards(tokens, routes, gate_num, w_gate, w_up, w_down):
    n = lax.axis_size("ep")
    rows, width = tokens.shape
    chips = n // SPLIT
    part = width // PARTS
    blocks = part // BLOCK
    group = min(chips, 8)
    half_rows = chips * CAP
    vmem = pl.BlockSpec(memory_space=pltpu.VMEM)
    hbm = pl.BlockSpec(memory_space=pltpu.HBM)
    sems = pltpu.SemaphoreType.DMA
    ret, mix = pl.pallas_call(
        functools.partial(kernel, n, group),
        out_shape=[
            jax.ShapeDtypeStruct((PARTS, chips, TILE, BLOCK), BF16),
            jax.ShapeDtypeStruct((blocks * rows, chips * TILE), BF16),
        ],
        in_specs=[vmem] * 3 + [hbm] * 3,
        out_specs=[vmem, vmem],
        scratch_shapes=[
            pltpu.VMEM(w_gate.shape[1:], BF16),
            pltpu.VMEM(w_up.shape[1:], BF16),
            pltpu.VMEM(w_down.shape[1:], BF16),
            pltpu.VMEM((PARTS, chips, TILE, BLOCK), BF16),
            pltpu.VMEM((PARTS, chips, TILE, BLOCK), BF16),
            pltpu.VMEM((PARTS, chips, TILE, BLOCK), BF16),
            pltpu.VMEM((PARTS, half_rows, part), F32),
            pltpu.VMEM((PARTS, half_rows, part), F32),
            pltpu.VMEM((PARTS, half_rows, part), F32),
            pltpu.VMEM((PARTS, chips, TILE, BLOCK), BF16),
            pltpu.VMEM((blocks * group * CAP, group * TILE), BF16),
            pltpu.VMEM((group * TILE, blocks * group * CAP), BF16),
            sems((3,)),
            sems((PARTS, chips)), sems((PARTS, chips)),
            sems((PARTS, chips)), sems((PARTS, chips)),
            sems((PARTS,)), sems((PARTS,)),
            sems((PARTS, chips)), sems((PARTS, chips)),
        ],
        compiler_params=pltpu.CompilerParams(
            collective_id=0, has_side_effects=True, vmem_limit_bytes=52 << 20
        ),
    )(tokens, routes.T, gate_num.T, w_gate, w_up, w_down)
    return pl.pallas_call(
        combine,
        out_shape=jax.ShapeDtypeStruct((rows, width), BF16),
        in_specs=[vmem, vmem],
        out_specs=vmem,
    )(ret, mix)


def solution(mesh):
    return jax.shard_map(
        shards,
        mesh=mesh,
        in_specs=(
            P(("groups", "ep"), None),
            P(("groups", "ep"), None),
            P(("groups", "ep"), None),
            P("ep", None, None),
            P("ep", None, None),
            P("ep", None, None),
        ),
        out_specs=P(("groups", "ep"), None),
        check_vma=False,
    )
```

time: 23.4 us -> 26.6 us (1.14)
  local copies, waits for them, and re-layouts: 0 us -> 3.57 us
  Pallas kernels: 23.3 us -> 22.8 us
    unnamed x0 -> x10, local copies, waits for them, and re-layouts: none -> 3.57 us
    pallas_call x1, Pallas kernels: 21.5 us -> 21 us  [shards(): pl.pallas_call(functools.partial(kernel, n, group), out_shape=[jax.ShapeD...]
where the time goes in v3:
time: 26.6 us; the launch traced here: 26.4 us
  Pallas kernels  22.8 us (86%)
  local copies, waits for them, and re-layouts  3.57 us (13%)
    pallas_call x1, Pallas kernels, shards(): pl.pallas_call(functools.partial(kernel, n, group), out_shape=[jax.ShapeD...  21 us
    unnamed x10, local copies, waits for them, and re-layouts  3.57 us
    pallas_call x1, Pallas kernels, shards(): pl.pallas_call(combine, out_shape=jax.ShapeDtypeStruct((rows, width), BF1...  1.8 us

profile of v3, /device:TPU:0, one launch (start us, length us, event | category | flops | bytes accessed | tf_op | source)
XLA Modules:
  0.0 26.4 jit_solution(12136994767173699190)
XLA Ops:
  0.0 0.0 copy-start
  0.0 0.9 %copy-done = bf16[32,3584]{1,0:T(8,128)(2,1)S(1)} copy-done((bf16[32,3584]{1,0:T(8,128)(2,1)S(1)}, bf16[32,3584]{1,0:T(8,128)(2,1)}, u32[]{:S(2)}) %copy-start) | copy-done | bytes 229400
  0.9 0.0 copy-start.3
  0.9 0.7 %copy-done.3 = s32[32,8]{0,1:T(8,128)S(1)} copy-done((s32[32,8]{0,1:T(8,128)S(1)}, s32[32,8]{0,1:T(8,128)}, u32[]{:S(2)}) %copy-start.3) | copy-done | bytes 1048
  1.6 0.0 copy-start.4
  1.6 0.7 %copy-done.4 = s32[32,8]{0,1:T(8,128)S(1)} copy-done((s32[32,8]{0,1:T(8,128)S(1)}, s32[32,8]{0,1:T(8,128)}, u32[]{:S(2)}) %copy-start.4) | copy-done | bytes 1048
  2.3 21.0 %shard_map.64 = (bf16[2,8,16,256]{3,2,1,0:T(8,128)(2,1)S(1)}, bf16[224,128]{1,0:T(8,128)(2,1)S(1)}) custom-call(bf16[32,3584]{1,0:T(8,128)(2,1)S(1)} %copy-done, s32[8,32]{1,0:T(8,128)S(1)} %bitcast.2, s32[8,32]{1,0:T(8,128)S(1)} %bitcast.3, bf16[1,3584,512]{2,1,0:T(8,128)(2,1)} %wg_hbm.1, bf16[1,3584,512]{2,1,0:T(8,128)(2,1)} %wu_hbm.1, ...), custom_call_target="tpu_custom_call" | custom-call | tf_op jit(solution)/shard_map/pallas_call | solution.py:269
  23.3 0.0 copy-start.1
  23.3 0.6 %copy-done.1 = bf16[2,8,16,256]{3,2,1,0:T(8,128)(2,1)} copy-done((bf16[2,8,16,256]{3,2,1,0:T(8,128)(2,1)}, bf16[2,8,16,256]{3,2,1,0:T(8,128)(2,1)S(1)}, u32[]{:S(2)}) %copy-start.1) | copy-done | bytes 131096
  24.0 0.0 copy-start.2
  24.0 0.6 %copy-done.2 = bf16[224,128]{1,0:T(8,128)(2,1)} copy-done((bf16[224,128]{1,0:T(8,128)(2,1)}, bf16[224,128]{1,0:T(8,128)(2,1)S(1)}, u32[]{:S(2)}) %copy-start.2) | copy-done | bytes 57368
  24.6 1.8 %shard_map.65 = bf16[32,3584]{1,0:T(8,128)(2,1)} custom-call(bf16[2,8,16,256]{3,2,1,0:T(8,128)(2,1)} %copy-done.1, bf16[224,128]{1,0:T(8,128)(2,1)} %copy-done.2), custom_call_target="tpu_custom_call" | custom-call | tf_op jit(solution)/shard_map/pallas_call | solution.py:300
Async XLA Ops:
  0.0 0.9 %copy-start = (bf16[32,3584]{1,0:T(8,128)(2,1)S(1)}, bf16[32,3584]{1,0:T(8,128)(2,1)}, u32[]{:S(2)}) copy-start(bf16[32,3584]{1,0:T(8,128)(2,1)} %tokens.1) | copy-start | bytes 688132
  0.9 0.7 %copy-start.3 = (s32[32,8]{0,1:T(8,128)S(1)}, s32[32,8]{0,1:T(8,128)}, u32[]{:S(2)}) copy-start(s32[32,8]{0,1:T(8,128)} %param.7) | copy-start | bytes 3076
  1.6 0.7 %copy-start.4 = (s32[32,8]{0,1:T(8,128)S(1)}, s32[32,8]{0,1:T(8,128)}, u32[]{:S(2)}) copy-start(s32[32,8]{0,1:T(8,128)} %param.8) | copy-start | bytes 3076
  23.3 0.6 %copy-start.1 = (bf16[2,8,16,256]{3,2,1,0:T(8,128)(2,1)}, bf16[2,8,16,256]{3,2,1,0:T(8,128)(2,1)S(1)}, u32[]{:S(2)}) copy-start(bf16[2,8,16,256]{3,2,1,0:T(8,128)(2,1)S(1)} %get-tuple-element.7.ret) | copy-start | bytes 393220
  24.0 0.6 %copy-start.2 = (bf16[224,128]{1,0:T(8,128)(2,1)}, bf16[224,128]{1,0:T(8,128)(2,1)S(1)}, u32[]{:S(2)}) copy-start(bf16[224,128]{1,0:T(8,128)(2,1)S(1)} %get-tuple-element.8.mix) | copy-start | bytes 172036

commit v4 on v3

--- a/solution.py
+++ b/solution.py
@@ -48,8 +48,9 @@
 
 
 def kernel(
-    n, group, tokens, routes, gates, wg_hbm, wu_hbm, wd_hbm, ret, mix,
-    wg, wu, wd, send, recv, relayed, kept, zsend, zrecv, rsend, gather, scatter, wsem, send_s, send_r, relay_s, relay_r, z_s, z_r, ret_s, ret_r,
+    n, group, tokens_hbm, routes, gates, wg_hbm, wu_hbm, wd_hbm, out,
+    tokens, wg, wu, wd, send, recv, relayed, kept, zsend, zrecv, rsend, ret, gather, scatter,
+    mix, rows_s, wsem, send_s, send_r, relay_s, relay_r, z_s, z_r, ret_s, ret_r,
 ):
     me = lax.axis_index("ep")
     side = lax.rem(me, SPLIT)
@@ -89,11 +90,12 @@
     others(greet)
     pl.semaphore_signal(barrier, inc=1, device_id={"ep": partner}, device_id_type=MESH)
 
+    fetch = pltpu.make_async_copy(tokens_hbm, tokens, rows_s)
     loads = [
         pltpu.make_async_copy(src.at[0], dst, wsem.at[i])
         for i, (src, dst) in enumerate(((wg_hbm, wg), (wu_hbm, wu), (wd_hbm, wd)))
     ]
-    for load in loads:
+    for load in [fetch] + loads:
         load.start()
 
     shape = (rows, tiled_rows)
@@ -140,6 +142,7 @@
             recv_sem=relay_r.at[h, q], device_id={"ep": partner}, device_id_type=MESH,
         )
 
+    fetch.wait()
     for h in range(PARTS):
         stacked = jnp.concatenate(
             [tokens[:, h * part + b * BLOCK : h * part + (b + 1) * BLOCK] for b in range(blocks)],
@@ -240,19 +243,12 @@
         exchange(h).wait_send()
     for h in range(PARTS):
         others(lambda q: given(h, q).wait_recv(), back=True)
-    for h in range(PARTS):
-        others(lambda q: give_back(h, q).wait_send())
-
-
-def combine(ret, mix, out):
-    rows = out.shape[0]
-    chips = ret.shape[1]
-    part = out.shape[1] // PARTS
-    for h in range(PARTS):
-        tall = mm(mix[...], ret[h].reshape(chips * TILE, BLOCK)).astype(BF16)
-        for b in range(part // BLOCK):
+        tall = mm(mix[...], ret[h].reshape(packet_rows, BLOCK)).astype(BF16)
+        for b in range(blocks):
             at = h * part + b * BLOCK
             out[:, at : at + BLOCK] = tall[b * rows : (b + 1) * rows]
+    for h in range(PARTS):
+        others(lambda q: give_back(h, q).wait_send())
 
 
 def shards(tokens, routes, gate_num, w_gate, w_up, w_down):
@@ -264,17 +260,15 @@
     group = min(chips, 8)
     half_rows = chips * CAP
     vmem = pl.BlockSpec(memory_space=pltpu.VMEM)
-    hbm = pl.BlockSpec(memory_space=pltpu.HBM)
+    hbm = pl.BlockSpec(memory_space=pl.ANY)
     sems = pltpu.SemaphoreType.DMA
-    ret, mix = pl.pallas_call(
+    return pl.pallas_call(
         functools.partial(kernel, n, group),
-        out_shape=[
-            jax.ShapeDtypeStruct((PARTS, chips, TILE, BLOCK), BF16),
-            jax.ShapeDtypeStruct((blocks * rows, chips * TILE), BF16),
-        ],
-        in_specs=[vmem] * 3 + [hbm] * 3,
-        out_specs=[vmem, vmem],
+        out_shape=jax.ShapeDtypeStruct((rows, width), BF16),
+        in_specs=[hbm, vmem, vmem, hbm, hbm, hbm],
+        out_specs=vmem,
         scratch_shapes=[
+            pltpu.VMEM((rows, width), BF16),
             pltpu.VMEM(w_gate.shape[1:], BF16),
             pltpu.VMEM(w_up.shape[1:], BF16),
             pltpu.VMEM(w_down.shape[1:], BF16),
@@ -285,8 +279,11 @@
             pltpu.VMEM((PARTS, half_rows, part), F32),
             pltpu.VMEM((PARTS, half_rows, part), F32),
             pltpu.VMEM((PARTS, chips, TILE, BLOCK), BF16),
+            pltpu.VMEM((PARTS, chips, TILE, BLOCK), BF16),
             pltpu.VMEM((blocks * group * CAP, group * TILE), BF16),
             pltpu.VMEM((group * TILE, blocks * group * CAP), BF16),
+            pltpu.VMEM((blocks * rows, chips * TILE), BF16),
+            sems,
             sems((3,)),
             sems((PARTS, chips)), sems((PARTS, chips)),
             sems((PARTS, chips)), sems((PARTS, chips)),
@@ -294,16 +291,9 @@
             sems((PARTS, chips)), sems((PARTS, chips)),
         ],
         compiler_params=pltpu.CompilerParams(
-            collective_id=0, has_side_effects=True, vmem_limit_bytes=52 << 20
+            collective_id=0, has_side_effects=True, vmem_limit_bytes=54800 << 10
         ),
     )(tokens, routes.T, gate_num.T, w_gate, w_up, w_down)
-    return pl.pallas_call(
-        combine,
-        out_shape=jax.ShapeDtypeStruct((rows, width), BF16),
-        in_specs=[vmem, vmem],
-        out_specs=vmem,
-    )(ret, mix)
-
 
 def solution(mesh):
     return jax.shard_map(

time: 26.6 us -> 23.8 us (0.89)
  local copies, waits for them, and re-layouts: 3.57 us -> 2.06 us
  Pallas kernels: 22.8 us -> 21.5 us
    unnamed x10 -> x5, local copies, waits for them, and re-layouts: 3.57 us -> 2.06 us
    pallas_call x2 -> x1, Pallas kernels: 22.8 us -> 21.5 us  [shards(): pl.pallas_call(functools.partial(kernel, n, group), out_shape=jax.ShapeDt...]
where the time goes in v4:
time: 23.8 us; the launch traced here: 23.6 us
  Pallas kernels  21.5 us (90%)
  local copies, waits for them, and re-layouts  2.06 us (9%)
    pallas_call x1, Pallas kernels, shards(): pl.pallas_call(functools.partial(kernel, n, group), out_shape=jax.ShapeDt...  21.5 us
    unnamed x5, local copies, waits for them, and re-layouts  2.06 us

profile of v4, /device:TPU:0, one launch (start us, length us, event | category | flops | bytes accessed | tf_op | source)
XLA Modules:
  0.0 23.6 jit_solution(2658168796260670690)
XLA Ops:
  0.0 0.0 copy-start
  0.0 0.7 %copy-done = s32[32,8]{0,1:T(8,128)S(1)} copy-done((s32[32,8]{0,1:T(8,128)S(1)}, s32[32,8]{0,1:T(8,128)}, u32[]{:S(2)}) %copy-start) | copy-done | bytes 1048
  0.7 0.0 copy-start.1
  0.7 0.7 %copy-done.1 = s32[32,8]{0,1:T(8,128)S(1)} copy-done((s32[32,8]{0,1:T(8,128)S(1)}, s32[32,8]{0,1:T(8,128)}, u32[]{:S(2)}) %copy-start.1) | copy-done | bytes 1048
  1.4 21.5 %shard_map.64 = bf16[32,3584]{1,0:T(8,128)(2,1)S(1)} custom-call(bf16[32,3584]{1,0:T(8,128)(2,1)} %tokens_hbm.1, s32[8,32]{1,0:T(8,128)S(1)} %bitcast.2, s32[8,32]{1,0:T(8,128)S(1)} %bitcast.3, bf16[1,3584,512]{2,1,0:T(8,128)(2,1)} %wg_hbm.1, bf16[1,3584,512]{2,1,0:T(8,128)(2,1)} %wu_hbm.1, bf16[1,512,3584]{2,1,0:T(8,128)(2,1)} %wd_hbm.1), custom_call_target="tpu_custom_call" | custom-call | tf_op jit(solution)/shard_map/pallas_call | solution.py:265
  22.9 0.7 %copy.8 = bf16[32,3584]{1,0:T(8,128)(2,1)} copy(bf16[32,3584]{1,0:T(8,128)(2,1)S(1)} %shard_map.64) | data formatting | bytes 458752
Async XLA Ops:
  0.0 0.7 %copy-start = (s32[32,8]{0,1:T(8,128)S(1)}, s32[32,8]{0,1:T(8,128)}, u32[]{:S(2)}) copy-start(s32[32,8]{0,1:T(8,128)} %param.7) | copy-start | bytes 3076
  0.7 0.7 %copy-start.1 = (s32[32,8]{0,1:T(8,128)S(1)}, s32[32,8]{0,1:T(8,128)}, u32[]{:S(2)}) copy-start(s32[32,8]{0,1:T(8,128)} %param.8) | copy-start | bytes 3076

commit v5 on v4

--- a/solution.py
+++ b/solution.py
@@ -48,7 +48,7 @@
 
 
 def kernel(
-    n, group, tokens_hbm, routes, gates, wg_hbm, wu_hbm, wd_hbm, out,
+    n, group, tokens_hbm, codes, wg_hbm, wu_hbm, wd_hbm, out,
     tokens, wg, wu, wd, send, recv, relayed, kept, zsend, zrecv, rsend, ret, gather, scatter,
     mix, rows_s, wsem, send_s, send_r, relay_s, relay_r, z_s, z_r, ret_s, ret_r,
 ):
@@ -57,7 +57,7 @@
     here = me // SPLIT
     partner = me + 1 - 2 * side
     rows, width = tokens.shape
-    top = routes.shape[0]
+    top = codes.shape[0]
     part = width // PARTS
     blocks = part // BLOCK
     chips = n // SPLIT
@@ -95,8 +95,7 @@
         pltpu.make_async_copy(src.at[0], dst, wsem.at[i])
         for i, (src, dst) in enumerate(((wg_hbm, wg), (wu_hbm, wu), (wd_hbm, wd)))
     ]
-    for load in [fetch] + loads:
-        load.start()
+    fetch.start()
 
     shape = (rows, tiled_rows)
     token_of = mod(iota(shape, 1), rows)
@@ -111,7 +110,7 @@
     shape = (slots, tiled_rows)
     expert_of = over(iota(shape, 0), CAP).astype(F32)
     copy_of = mod(iota(shape, 0), CAP).astype(F32)
-    ints = jnp.concatenate([routes[...], gates[...]], axis=0).astype(F32).astype(BF16)
+    ints = jnp.concatenate([codes[...] >> 8, codes[...] & 255], axis=0).astype(F32).astype(BF16)
     tiled = mm(ints, repeat)
     named = jnp.zeros(shape, F32)
     weight = jnp.zeros(shape, F32)
@@ -143,6 +142,8 @@
         )
 
     fetch.wait()
+    for load in loads:
+        load.start()
     for h in range(PARTS):
         stacked = jnp.concatenate(
             [tokens[:, h * part + b * BLOCK : h * part + (b + 1) * BLOCK] for b in range(blocks)],
@@ -259,13 +260,14 @@
     blocks = part // BLOCK
     group = min(chips, 8)
     half_rows = chips * CAP
+    codes = routes.T * 256 + gate_num.T
     vmem = pl.BlockSpec(memory_space=pltpu.VMEM)
     hbm = pl.BlockSpec(memory_space=pl.ANY)
     sems = pltpu.SemaphoreType.DMA
     return pl.pallas_call(
         functools.partial(kernel, n, group),
         out_shape=jax.ShapeDtypeStruct((rows, width), BF16),
-        in_specs=[hbm, vmem, vmem, hbm, hbm, hbm],
+        in_specs=[hbm, vmem, hbm, hbm, hbm],
         out_specs=vmem,
         scratch_shapes=[
             pltpu.VMEM((rows, width), BF16),
@@ -293,7 +295,7 @@
         compiler_params=pltpu.CompilerParams(
             collective_id=0, has_side_effects=True, vmem_limit_bytes=54800 << 10
         ),
-    )(tokens, routes.T, gate_num.T, w_gate, w_up, w_down)
+    )(tokens, codes, w_gate, w_up, w_down)
 
 def solution(mesh):
     return jax.shard_map(

time: 23.8 us -> 22.9 us (0.962)
  local copies, waits for them, and re-layouts: 2.06 us -> 0.69 us
  other arithmetic: 0 us -> 0.71 us
    unnamed x5 -> x1, local copies, waits for them, and re-layouts: 2.06 us -> 0.69 us
    add x0 -> x1, other arithmetic: none -> 0.71 us  [shards(): codes = routes.T * 256 + gate_num.T]
    pallas_call x1, Pallas kernels: 21.5 us -> 21.3 us  [shards(): pl.pallas_call(functools.partial(kernel, n, group), out_shape=jax.ShapeDt...]
where the time goes in v5:
time: 22.9 us; the launch traced here: 22.7 us
  Pallas kernels  21.3 us (93%)
  other arithmetic  0.71 us (3%)
  local copies, waits for them, and re-layouts  0.69 us (3%)
    pallas_call x1, Pallas kernels, shards(): pl.pallas_call(functools.partial(kernel, n, group), out_shape=jax.ShapeDt...  21.3 us
    add x1, other arithmetic, shards(): codes = routes.T * 256 + gate_num.T  0.71 us
    unnamed x1, local copies, waits for them, and re-layouts  0.69 us

profile of v5, /device:TPU:0, one launch (start us, length us, event | category | flops | bytes accessed | tf_op | source)
XLA Modules:
  0.0 22.7 jit_solution(11199675281291227284)
XLA Ops:
  0.0 0.7 %add_bitcast_fusion.codes = s32[8,32]{1,0:T(8,128)S(1)} fusion(s32[32,8]{0,1:T(8,128)} %param.8, s32[32,8]{0,1:T(8,128)} %param.7), kind=kLoop, calls=%fused_computation | loop fusion | flops 512 | bytes 3072 | tf_op jit(solution)/shard_map/add | solution.py:263
  0.7 21.3 %shard_map.64 = bf16[32,3584]{1,0:T(8,128)(2,1)S(1)} custom-call(bf16[32,3584]{1,0:T(8,128)(2,1)} %tokens_hbm.1, s32[8,32]{1,0:T(8,128)S(1)} %add_bitcast_fusion.codes, bf16[1,3584,512]{2,1,0:T(8,128)(2,1)} %wg_hbm.1, bf16[1,3584,512]{2,1,0:T(8,128)(2,1)} %wu_hbm.1, bf16[1,512,3584]{2,1,0:T(8,128)(2,1)} %wd_hbm.1), custom_call_target="tpu_custom_call" | custom-call | tf_op jit(solution)/shard_map/pallas_call | solution.py:267
  22.0 0.7 %copy.8 = bf16[32,3584]{1,0:T(8,128)(2,1)} copy(bf16[32,3584]{1,0:T(8,128)(2,1)S(1)} %shard_map.64) | data formatting | bytes 458752

commit v6 on v5

--- a/solution.py
+++ b/solution.py
@@ -217,12 +217,12 @@
     loads[2].wait()
     for h in range(PARTS):
         z = mm(hidden, wd[:, h * part : (h + 1) * part])
-        zsend[h] = z[half_rows:]
+        zsend[h] = z[half_rows:].astype(BF16)
         exchange(h).start()
         kept[h] = z[:half_rows]
     for h in range(PARTS):
         exchange(h).wait_recv()
-        total = (kept[h] + zrecv[h]).astype(BF16)
+        total = (kept[h] + zrecv[h].astype(F32)).astype(BF16)
         for g in range(chips // group):
             lines = slice(g * group * CAP, (g + 1) * group * CAP)
             tall = jnp.concatenate(
@@ -278,8 +278,8 @@
             pltpu.VMEM((PARTS, chips, TILE, BLOCK), BF16),
             pltpu.VMEM((PARTS, chips, TILE, BLOCK), BF16),
             pltpu.VMEM((PARTS, half_rows, part), F32),
-            pltpu.VMEM((PARTS, half_rows, part), F32),
-            pltpu.VMEM((PARTS, half_rows, part), F32),
+            pltpu.VMEM((PARTS, half_rows, part), BF16),
+            pltpu.VMEM((PARTS, half_rows, part), BF16),
             pltpu.VMEM((PARTS, chips, TILE, BLOCK), BF16),
             pltpu.VMEM((PARTS, chips, TILE, BLOCK), BF16),
             pltpu.VMEM((blocks * group * CAP, group * TILE), BF16),

time: 22.9 us -> 22.8 us (level)
  no operation moved by 1% of the time
where the time goes in v6:
time: 22.8 us; the launch traced here: 22.6 us
  Pallas kernels  21.2 us (93%)
  other arithmetic  0.71 us (3%)
  local copies, waits for them, and re-layouts  0.69 us (3%)
    pallas_call x1, Pallas kernels, shards(): pl.pallas_call(functools.partial(kernel, n, group), out_shape=jax.ShapeDt...  21.2 us
    add x1, other arithmetic, shards(): codes = routes.T * 256 + gate_num.T  0.71 us
    unnamed x1, local copies, waits for them, and re-layouts  0.69 us

profile of v6, /device:TPU:0, one launch (start us, length us, event | category | flops | bytes accessed | tf_op | source)
XLA Modules:
  0.0 22.6 jit_solution(5596946792246726092)
XLA Ops:
  0.0 0.7 %add_bitcast_fusion.codes = s32[8,32]{1,0:T(8,128)S(1)} fusion(s32[32,8]{0,1:T(8,128)} %param.8, s32[32,8]{0,1:T(8,128)} %param.7), kind=kLoop, calls=%fused_computation | loop fusion | flops 512 | bytes 3072 | tf_op jit(solution)/shard_map/add | solution.py:263
  0.7 21.2 %shard_map.64 = bf16[32,3584]{1,0:T(8,128)(2,1)S(1)} custom-call(bf16[32,3584]{1,0:T(8,128)(2,1)} %tokens_hbm.1, s32[8,32]{1,0:T(8,128)S(1)} %add_bitcast_fusion.codes, bf16[1,3584,512]{2,1,0:T(8,128)(2,1)} %wg_hbm.1, bf16[1,3584,512]{2,1,0:T(8,128)(2,1)} %wu_hbm.1, bf16[1,512,3584]{2,1,0:T(8,128)(2,1)} %wd_hbm.1), custom_call_target="tpu_custom_call" | custom-call | tf_op jit(solution)/shard_map/pallas_call | solution.py:267
  21.9 0.7 %copy.8 = bf16[32,3584]{1,0:T(8,128)(2,1)} copy(bf16[32,3584]{1,0:T(8,128)(2,1)S(1)} %shard_map.64) | data formatting | bytes 458752
